TPU v7x, 32 devices: a whole 2x2x4 slice. The times are simulated.
32 devices in a mesh: grp: 2 (over y), dev: 4 (over z), tp: 4 (over x, core).
Axes of the slice: x: 2, y: 2, z: 4, core: 2. Of those that a mesh axis runs over, the one named last changes fastest.
Arguments:
- residual_input: bfloat16 [256, 6144], P(('grp', 'dev'), 'tp'), parts along dimension 0, may hold values from -32 to 32
- queries: bfloat16 [256, 6144], P(('grp', 'dev'), 'tp'), parts along dimension 0, may hold values from -6 to 6
- new_kv: bfloat16 [256, 2, 1024], P(('grp', 'dev'), None, 'tp'), parts along dimension 0, may hold values from -6 to 6
- cache: bfloat16 [256, 2, 64, 1024], P(('grp', 'dev'), None, None, 'tp'), parts along dimension 0, may hold values from -6 to 6
- lengths: int32 [256], P(('grp', 'dev')), parts along dimension 0, may hold values from 1 to 64, as said below
- slots: int32 [256], P(('grp', 'dev')), parts along dimension 0, may hold values from 0 to 31, as said below
- out_weight: bfloat16 [6144, 6144], P('tp', 'dev'), may hold values from -0.109375 to 0.109375
- norm_gain: float32 [6144], P('tp'), may hold values from 0.1 to 1.9
- router_weight: bfloat16 [6144, 4], P('tp'), may hold values from -0.078125 to 0.078125
- up_weight: bfloat16 [32768, 6144], P('dev', 'tp'), may hold values from -0.078125 to 0.078125
- down_weight: bfloat16 [32768, 6144], P('dev', 'tp'), may hold values from -0.0625 to 0.0625
- routes: int32 [256, 2], P(('grp', 'dev')), parts along dimension 0, may hold values from 0 to 3, all different within a row; in each aligned block of 32 rows (0 to 31, 32 to 63, ...) at most 24 rows name the same one
Outputs:
- layer_out: bfloat16 [256, 6144], P(('grp', 'dev'), 'tp'), parts along dimension 0
There are 2 independent parts, one for each index of `grp`. A program takes and returns all parts, laid end to end along the dimension named above; an argument that names none is the same for every part. Nothing has to cross between parts.
Inputs may be any that keep to these rules, and one draw needn't show every extreme that they name: `routes`: each row names two different experts; among the 32 rows of one index of dev no expert is named by more than 24 rows. `lengths`: each index of dev has a slot with all 64 positions valid. `slots`: each aligned block of 32 rows (the rows of one index of dev) names every slot 0 to 31 once.
All inputs are finite; a program needn't handle non-finite values.
Results may differ from a plain program's by a relative error of at most 0.005.
Values may be sent and summed in bfloat16 or wider, within the bound.
A program may use at most 128 MiB of HBM per device.

v0:
```python
import jax
import jax.numpy as jnp
from jax import lax
from jax.sharding import PartitionSpec as P

D = 6144
HEAD_DIM = 128
CAP = 24


eps = 1e-05


def sum_heads(terms):
    return lax.psum_scatter(terms, "tp", scatter_dimension=1, tiled=True)


def body(
    residual_input,
    queries,
    new_kv,
    cache,
    lengths,
    slots,
    out_weight,
    norm_gain,
    router_weight,
    up_weight,
    down_weight,
    routes,
):
    row_count = residual_input.shape[0]
    features = residual_input.shape[1]
    kv_local = cache.shape[3] // HEAD_DIM
    group = queries.shape[1] // cache.shape[3]
    positions = cache.shape[2]
    experts = router_weight.shape[1]
    devices = lax.axis_size("dev")
    pieces = devices // experts
    capacity = CAP
    placing = (slots[:, None] == lax.broadcasted_iota(jnp.int32, (row_count, row_count), 1)).astype(
        jnp.bfloat16
    )
    contract_rows = (((0,), (0,)), ((), ()))
    query_slot = lax.dot_general(
        placing, queries, contract_rows, preferred_element_type=jnp.float32
    ).astype(jnp.bfloat16)
    current_slot = lax.dot_general(
        placing, new_kv.reshape(row_count, -1), contract_rows, preferred_element_type=jnp.float32
    ).astype(jnp.bfloat16)
    current_slot = current_slot.reshape(row_count, 2, kv_local, HEAD_DIM)
    query_vector = query_slot.reshape(row_count, kv_local, group, HEAD_DIM)
    keys = cache[:, 0].reshape(row_count, positions, kv_local, HEAD_DIM)
    values = cache[:, 1].reshape(row_count, positions, kv_local, HEAD_DIM)
    scale = HEAD_DIM ** (-0.5)
    scores = (
        jnp.einsum("bkgd,blkd->bkgl", query_vector, keys, preferred_element_type=jnp.float32)
        * scale
    )
    own = (
        jnp.einsum(
            "orwm,orm->orw", query_vector, current_slot[:, 0], preferred_element_type=jnp.float32
        )
        * scale
    )
    mask = lax.broadcasted_iota(jnp.int32, (1, 1, 1, positions), 3) < lengths[:, None, None, None]
    scores = jnp.where(mask, scores, -jnp.inf)
    top = jnp.maximum(jnp.max(scores, -1), own)
    raised = jnp.exp(scores - top[..., None])
    own_raised = jnp.exp(own - top)
    total = jnp.sum(raised, -1) + own_raised
    probs = (raised / total[..., None]).astype(jnp.bfloat16)
    own_prob = (own_raised / total).astype(jnp.bfloat16)
    attended = jnp.einsum("bkgl,blkd->bkgd", probs, values, preferred_element_type=jnp.float32)
    attended = (
        attended
        + own_prob.astype(jnp.float32)[..., None]
        * current_slot[:, 1].astype(jnp.float32)[:, :, None, :]
    )
    attention_slot = attended.reshape(row_count, -1).astype(jnp.bfloat16)
    attention = jnp.dot(placing, attention_slot, preferred_element_type=jnp.float32).astype(
        jnp.bfloat16
    )
    partial_rows = jnp.dot(
        lax.all_gather(attention, "dev", axis=0, tiled=True),
        out_weight,
        preferred_element_type=jnp.float32,
    )
    terms = lax.all_to_all(partial_rows, "dev", split_axis=0, concat_axis=1, tiled=True)
    projected = sum_heads(terms)
    mixed = residual_input.astype(jnp.float32) + projected
    gained = mixed * norm_gain
    router = router_weight.astype(jnp.float32)
    square = lax.psum(jnp.sum(mixed * mixed, 1), "tp")
    scale_row = lax.rsqrt(square / D + eps)
    normed_wide = gained * scale_row[:, None]
    logits = lax.psum(jnp.dot(normed_wide, router, precision=lax.Precision.HIGHEST), "tp")
    normed = normed_wide.astype(jnp.bfloat16)
    expert_ids = lax.broadcasted_iota(jnp.int32, (row_count, experts), 1)
    first = (routes[:, 0:1] == expert_ids).astype(jnp.float32)
    second = (routes[:, 1:2] == expert_ids).astype(jnp.float32)
    first_logit = jnp.sum(logits * first, 1)
    second_logit = jnp.sum(logits * second, 1)
    first_gate = 1.0 / (1.0 + jnp.exp(second_logit - first_logit))
    second_gate = 1.0 / (1.0 + jnp.exp(first_logit - second_logit))
    row_weight_matrix = first * first_gate[:, None] + second * second_gate[:, None]
    member = first + second
    position = jnp.cumsum(member, 0) - member
    slot_grid = lax.broadcasted_iota(jnp.float32, (1, capacity, 1), 1)
    selection = member.T[:, None, :] * (position.T[:, None, :] == slot_grid).astype(jnp.float32)
    outgoing = jnp.einsum(
        "ecb,bf->ecf", selection.astype(jnp.bfloat16), normed, preferred_element_type=jnp.float32
    ).astype(jnp.bfloat16)
    outgoing = jnp.broadcast_to(outgoing[:, None], (experts, pieces, capacity, features)).reshape(
        devices, capacity, features
    )
    arrived = lax.all_to_all(outgoing, "dev", split_axis=0, concat_axis=0, tiled=True)
    count = arrived.shape[1]
    flat = arrived.reshape(devices * count, features)
    pre = lax.dot_general(
        flat, up_weight, (((1,), (1,)), ((), ())), preferred_element_type=jnp.float32
    )
    summed = lax.psum(pre, "tp")
    hidden = jax.nn.silu(summed).astype(jnp.bfloat16)
    part = jnp.dot(hidden, down_weight, preferred_element_type=jnp.float32).astype(jnp.bfloat16)
    returned = lax.all_to_all(
        part.reshape(devices, count, features), "dev", split_axis=0, concat_axis=0, tiled=True
    )
    expert_sum = jnp.sum(
        returned.reshape(experts, pieces, capacity, features).astype(jnp.float32), 1
    )
    placed = selection * row_weight_matrix.T[:, None, :]
    moe = jnp.einsum("ecb,ecf->bf", placed, expert_sum, precision=lax.Precision.HIGHEST)
    return (mixed + moe).astype(jnp.bfloat16)


def solution(mesh):
    in_specs = (
        P(("grp", "dev"), "tp"),
        P(("grp", "dev"), "tp"),
        P(("grp", "dev"), None, "tp"),
        P(("grp", "dev"), None, None, "tp"),
        P(("grp", "dev")),
        P(("grp", "dev")),
        P("tp", "dev"),
        P("tp"),
        P("tp", None),
        P("dev", "tp"),
        P("dev", "tp"),
        P(("grp", "dev"), None),
    )
    out_specs = P(("grp", "dev"), "tp")
    return jax.shard_map(body, mesh=mesh, in_specs=in_specs, out_specs=out_specs, check_vma=False)
```

profile of v0, /device:TPU:0, one launch (start us, length us, event | category | flops | bytes accessed | tf_op | source)
XLA Modules:
  0.0 226.7 jit_solution(3902782942847689107)
XLA Ops:
  6.5 0.8 iota_compare_fusion.4
  7.3 0.8 copy.28
  8.1 0.9 convolution_convert_fusion.4
  9.0 0.9 convolution_convert_fusion.3
  10.0 0.1 reshape.164
  10.1 1.7 fusion.36
  11.8 0.3 reshape_squeeze.6
  12.1 0.2 fusion.18
  12.3 0.8 fusion.37
  13.1 0.3 fusion.7
  13.5 0.3 reshape_squeeze.7
  13.8 0.5 fusion.4
  14.2 0.1 convert_element_type.90
  14.4 0.2 convolution_convert_fusion.2
  14.6 16.2 %all_gather.3 = bf16[128,1536]{1,0:T(8,128)(2,1)S(1)} all-gather(bf16[32,1536]{1,0:T(8,128)(2,1)S(1)} %convolution_convert_fusion.2), channel_id=1, replica_groups=mesh['grp'=2,'dev'=4,'tp'=4] {'dev'}, dimensions={0}, use_global_device_ids=true | all-gather | bytes 491520 | tf_op jit(solution)/shard_map/all_gather | solution.py:85
  30.9 3.1 %fusion.38 = f32[128,1536]{1,0:T(8,128)S(1)} fusion(bf16[128,1536]{1,0:T(8,128)(2,1)S(1)} %all_gather.3, bf16[1536,1536]{1,0:T(8,128)(2,1)} %param.18), kind=kOutput, calls=%fused_computation.76 | convolution fusion | flops 603979776 | bytes 5898240 | tf_op jit(solution)/shard_map/dot_general | solution.py:84
  34.0 21.8 %all_to_all.29 = f32[4,32,1536]{2,1,0:T(8,128)S(1)} all-to-all(f32[4,32,1536]{2,1,0:T(8,128)S(1)} %bitcast.51), channel_id=1, replica_groups=mesh['grp'=2,'dev'=4,'tp'=4] {'dev'}, dimensions={0} | all-to-all | bytes 1572864 | tf_op jit(solution)/shard_map/all_to_all | solution.py:89
  55.8 0.9 copy.27
  56.9 22.5 %reduce-scatter.2.cloned.1.call-done = f32[32,1536]{1,0:T(8,128)} async-done(((f32[32,6144]{1,0:T(8,128)}), f32[32,1536]{1,0:T(8,128)}) %reduce-scatter.2.cloned.1.call-update) | async-done | bytes 196624 | tf_op jit(solution)/shard_map/reduce_scatter | solution.py:15
  79.3 1.1 multiply_reduce_fusion
  80.4 5.8 %psum.21 = f32[32]{0:T(128)S(1)} all-reduce(f32[32]{0:T(128)S(1)} %multiply_reduce_fusion), channel_id=1, replica_groups=mesh['grp'=2,'dev'=4,'tp'=4] {'tp'}, use_global_device_ids=true, to_apply=%region_5.6 | all-reduce | flops 32 | bytes 256 | tf_op jit(solution)/shard_map/psum | solution.py:94
  86.2 1.1 fusion.9
  87.3 5.7 %psum.22 = f32[32,4]{0,1:T(4,128)S(1)} all-reduce(f32[32,4]{0,1:T(4,128)S(1)} %fusion.9), channel_id=1, replica_groups=mesh['grp'=2,'dev'=4,'tp'=4] {'tp'}, use_global_device_ids=true, to_apply=%region_6.7 | all-reduce | flops 128 | bytes 1024 | tf_op jit(solution)/shard_map/psum | solution.py:97
  93.2 0.1 select_add_fusion
  93.5 1.2 convolution_convert_fusion
  94.7 14.2 %all_to_all.30 = bf16[4,24,1536]{2,1,0:T(8,128)(2,1)S(1)} all-to-all(bf16[4,24,1536]{2,1,0:T(8,128)(2,1)S(1)} %convolution_convert_fusion), channel_id=1, replica_groups=mesh['grp'=2,'dev'=4,'tp'=4] {'dev'}, dimensions={0} | all-to-all | bytes 589824 | tf_op jit(solution)/shard_map/all_to_all | solution.py:117
  108.9 14.1 %fusion.39 = f32[96,8192]{1,0:T(8,128)} fusion(bf16[96,1536]{1,0:T(8,128)(2,1)S(1)} %bitcast.52, bf16[8192,1536]{1,0:T(8,128)(2,1)} %param.21), kind=kOutput, calls=%fused_computation.77 | convolution fusion | flops 2415919104 | bytes 28606464 | tf_op jit(solution)/shard_map/dot_general | solution.py:120
  123.1 67.6 %all-reduce.2.cloned.1.call-done = f32[96,8192]{1,0:T(8,128)} async-done(((f32[96,8192]{1,0:T(8,128)}), f32[96,8192]{1,0:T(8,128)}) %all-reduce.2.cloned.1.call-update) | async-done | bytes 3145744 | tf_op jit(solution)/shard_map/psum | solution.py:123
  190.7 14.1 %convolution_convert_fusion.1 = bf16[96,1536]{1,0:T(8,128)(2,1)} fusion(bf16[8192,1536]{1,0:T(8,128)(2,1)} %param.22, f32[96,8192]{1,0:T(8,128)} %all-reduce.2.cloned.1.call-done), kind=kOutput, calls=%fused_computation.2 | convolution fusion | flops 2419998720 | bytes 28606464 | tf_op jit(solution)/shard_map/dot_general | solution.py:125
  204.8 4.6 %all-to-all-start.2 = ((bf16[4,24,1536]{2,1,0:T(8,128)(2,1)}), bf16[4,24,1536]{2,1,0:T(8,128)(2,1)S(1)}, u32[]{:S(2)}, u32[]{:S(2)}) async-start(bf16[4,24,1536]{2,1,0:T(8,128)(2,1)} %bitcast.12), calls=%async_computation.3 | async-start | bytes 589824 | tf_op jit(solution)/shard_map/all_to_all | solution.py:126
  209.4 9.5 %all-to-all-done.2 = bf16[4,24,1536]{2,1,0:T(8,128)(2,1)S(1)} async-done(((bf16[4,24,1536]{2,1,0:T(8,128)(2,1)}), bf16[4,24,1536]{2,1,0:T(8,128)(2,1)S(1)}, u32[]{:S(2)}, u32[]{:S(2)}) %all-to-all-start.2) | async-done | bytes 294944 | tf_op jit(solution)/shard_map/all_to_all | solution.py:126
  218.9 1.0 fusion.1
  (33 shorter events, 0.7 us)
Async XLA Ops:
  6.5 2.5 %copy-start = (bf16[32,1536]{1,0:T(8,128)(2,1)S(1)}, bf16[32,1536]{1,0:T(8,128)(2,1)}, u32[]{:S(2)}) copy-start(bf16[32,1536]{1,0:T(8,128)(2,1)} %param.13) | copy-start | bytes 294916
  6.5 72.8 %reduce-scatter.2.cloned.1.call-start = ((), (), s32[]{:S(2)}) async-start(), calls=%async_computation.4 | async-start | bytes 983040 | tf_op jit(solution)/shard_map/reduce_scatter | solution.py:15
  13.8 0.7 copy-start.6
  34.0 22.9 %copy-start.7 = (s32[32,2]{0,1:T(2,128)S(1)}, s32[32,2]{0,1:T(2,128)}, u32[]{:S(2)}) copy-start(s32[32,2]{0,1:T(2,128)} %param.23) | copy-start | bytes 772
  34.0 45.3 %copy-start.3 = (bf16[32,1536]{1,0:T(8,128)(2,1)S(1)}, bf16[32,1536]{1,0:T(8,128)(2,1)}, u32[]{:S(2)}) copy-start(bf16[32,1536]{1,0:T(8,128)(2,1)} %param.12) | copy-start | bytes 294916
  34.0 52.2 %copy-start.4 = (f32[1536]{0:T(1024)S(1)}, f32[1536]{0:T(1024)}, u32[]{:S(2)}) copy-start(f32[1536]{0:T(1024)} %param.19) | copy-start | bytes 18436
  34.0 52.1 %copy-start.5 = (bf16[1536,4]{0,1:T(4,128)(2,1)S(1)}, bf16[1536,4]{0,1:T(4,128)(2,1)}, u32[]{:S(2)}) copy-start(bf16[1536,4]{0,1:T(4,128)(2,1)} %param.20) | copy-start | bytes 36868
  56.8 133.9 %all-reduce.2.cloned.1.call-start = ((), (), s32[]{:S(2)}) async-start(), calls=%async_computation.5 | async-start | bytes 6291456 | tf_op jit(solution)/shard_map/psum | solution.py:123
  123.0 95.8 %copy-start.2 = (f32[32,1536]{1,0:T(8,128)S(1)}, f32[32,1536]{1,0:T(8,128)}, u32[]{:S(2)}) copy-start(f32[32,1536]{1,0:T(8,128)} %reduce-scatter.2.cloned.1.call-done) | copy-start | bytes 589828
  190.7 29.2 %copy-start.1 = (bf16[32,1536]{1,0:T(8,128)(2,1)S(1)}, bf16[32,1536]{1,0:T(8,128)(2,1)}, u32[]{:S(2)}) copy-start(bf16[32,1536]{1,0:T(8,128)(2,1)} %param.13) | copy-start | bytes 294916
  204.8 14.1 %all-to-all-start.2 = ((bf16[4,24,1536]{2,1,0:T(8,128)(2,1)}), bf16[4,24,1536]{2,1,0:T(8,128)(2,1)S(1)}, u32[]{:S(2)}, u32[]{:S(2)}) async-start(bf16[4,24,1536]{2,1,0:T(8,128)(2,1)} %bitcast.12), calls=%async_computation.3 | async-start | bytes 589824 | tf_op jit(solution)/shard_map/all_to_all | solution.py:126
Sparse Core Ops, SparseCore 0:
  56.9 22.3 reduce-scatter.1
  123.2 67.4 all-reduce.1
where the time goes:
time: 227 us
  waiting for transfers between devices  99.6 us (44%)
  blocking collectives  63.7 us (28%)
  matrix products  38.1 us (17%)
  between operations  13.6 us (6%)
  local copies, waits for them, and re-layouts  4.66 us (2%)
  starting transfers between devices  4.62 us (2%)
  other arithmetic  2.39 us (1%)
    psum x1, waiting for transfers between devices, body(): summed = lax.psum(pre, 'tp')  67.6 us
    reduce_scatter x1, waiting for transfers between devices, sum_heads(): return lax.psum_scatter(terms, 'tp', scatter_dimension=1, tiled=True)  22.5 us
    all_to_all x1, blocking collectives, body(): lax.all_to_all(partial_rows, 'dev', split_axis=0, concat_axis=1, tiled=True)  21.8 us
    all_gather x1, blocking collectives, body(): lax.all_gather(attention, 'dev', axis=0, tiled=True)  16.2 us
    all_to_all x1, blocking collectives, body(): lax.all_to_all(outgoing, 'dev', split_axis=0, concat_axis=0, tiled=True)  14.2 us
    dot_general x1, matrix products, body(): lax.dot_general(flat, up_weight, (((1,), (1,)), ((), ())), preferred_elem...  14.1 us
    dot_general x1, matrix products, body(): jnp.dot(hidden, down_weight, preferred_element_type=jnp.float32)  14.1 us
    all_to_all x1, waiting for transfers between devices, body(): lax.all_to_all(part.reshape(devices, count, features), 'dev', split_axis=...  9.45 us
  transfers between devices with their start and end apart: 3, of which 3 were waited for; matrix products, arithmetic and copies ran while one was open for 0% of the time, Pallas kernels for 0%

commit v1 on v0

--- a/solution.py
+++ b/solution.py
@@ -1,6 +1,8 @@
 import jax
 import jax.numpy as jnp
 from jax import lax
+from jax.experimental import pallas as pl
+from jax.experimental.pallas import tpu as pltpu
 from jax.sharding import PartitionSpec as P
 
 D = 6144
@@ -9,6 +11,443 @@
 
 
 eps = 1e-05
+
+
+MESH = pl.DeviceIdType.MESH
+CHUNKS = 8
+NT = (((1,), (1,)), ((), ()))
+
+
+def send(source, target, send_sem, recv_sem, where):
+    return pltpu.make_async_remote_copy(
+        src_ref=source,
+        dst_ref=target,
+        send_sem=send_sem,
+        recv_sem=recv_sem,
+        device_id=where,
+        device_id_type=MESH,
+    )
+
+
+def fold(block):
+    half = block.shape[1] // 2
+    return jnp.concatenate([block[:, :half], block[:, half:]], 0).astype(jnp.bfloat16)
+
+
+def unfold(block):
+    rows = block.shape[0] // 2
+    wide = block.astype(jnp.float32)
+    return jnp.concatenate([wide[:rows], wide[rows:]], 1)
+
+
+def layer_kernel(
+    att_ref,
+    res_ref,
+    gain_ref,
+    router_ref,
+    routes_ref,
+    routes_t_ref,
+    outw_hbm,
+    up_hbm,
+    down_hbm,
+    out_ref,
+    weights,
+    outw,
+    gathered,
+    projected,
+    core_out,
+    core_in,
+    x_out,
+    x_in,
+    turn_out,
+    turn_in,
+    mixed_ref,
+    stat_out,
+    stat_in,
+    outgoing,
+    arrived,
+    flat_ref,
+    pair_out,
+    pair_in,
+    own_pre,
+    far_out,
+    far_in,
+    hid_own,
+    hid_in,
+    acc,
+    back_out,
+    back_in,
+    weight_sem,
+    outw_sem,
+    gather_sems,
+    hop_sems,
+    stat_sems,
+    there_sems,
+    back_sems,
+    pair_sems,
+    far_sems,
+    hid_sems,
+):
+    devices, row_count, features = gathered.shape
+    slots = weights.shape[0]
+    chunk = weights.shape[1]
+    half = chunk // 2
+    experts = router_ref.shape[0]
+    f32 = jnp.float32
+    bf16 = jnp.bfloat16
+    d = lax.axis_index("dev")
+    t = lax.axis_index("tp")
+    core = lax.rem(t, 2)
+    x = t // 2
+    sibling = x * 2 + (1 - core)
+    far = (1 - x) * 2 + core
+
+    def up_copy(k):
+        return pltpu.make_async_copy(
+            up_hbm.at[pl.ds(k * chunk, chunk)], weights.at[k], weight_sem.at[k]
+        )
+
+    def down_copy(k):
+        return pltpu.make_async_copy(
+            down_hbm.at[pl.ds(k * chunk, chunk)],
+            weights.at[lax.rem(k + CHUNKS, slots)],
+            weight_sem.at[k + CHUNKS],
+        )
+
+    outw_copy = pltpu.make_async_copy(outw_hbm, outw, outw_sem)
+    outw_copy.start()
+    for k in range(CHUNKS):
+        up_copy(k).start()
+    for k in range(slots - CHUNKS):
+        down_copy(k).start()
+
+    barrier = pltpu.get_barrier_semaphore()
+    for off in range(1, 4):
+        pl.semaphore_signal(
+            barrier, inc=1, device_id={"dev": lax.rem(d + off, 4)}, device_id_type=MESH
+        )
+        pl.semaphore_signal(
+            barrier, inc=1, device_id={"tp": lax.rem(t + off, 4)}, device_id_type=MESH
+        )
+
+    @pl.when(d != t)
+    def _():
+        pl.semaphore_signal(barrier, inc=1, device_id={"dev": t, "tp": d}, device_id_type=MESH)
+        pl.semaphore_wait(barrier, 7)
+
+    @pl.when(d == t)
+    def _():
+        pl.semaphore_wait(barrier, 6)
+
+    copies = []
+    for off in range(1, 4):
+        copy = send(
+            att_ref,
+            gathered.at[d],
+            gather_sems.at[0, off],
+            gather_sems.at[1, off],
+            {"dev": lax.rem(d + off, 4)},
+        )
+        copy.start()
+        copies.append(copy)
+    gathered[d] = att_ref[...]
+    outw_copy.wait()
+    for copy in copies:
+        copy.wait()
+
+    rows_all = gathered[...].reshape(devices * row_count, features)
+
+    @pl.loop(0, 3)
+    def _(j):
+        cols = pl.ds(pl.multiple_of(j * 512, 512), 512)
+        projected[:, :, cols] = jnp.dot(
+            rows_all, outw[:, cols], preferred_element_type=f32
+        ).reshape(devices, row_count, 512)
+
+    core_out[0] = projected[1 - core].astype(bf16)
+    core_out[1] = projected[3 - core].astype(bf16)
+    copy_core = send(core_out, core_in, hop_sems.at[0], hop_sems.at[1], {"tp": sibling})
+    copy_core.start()
+    copy_core.wait()
+    x_out[...] = (projected[far] + core_in[1 - x].astype(f32)).astype(bf16)
+    copy_x = send(x_out, x_in, hop_sems.at[2], hop_sems.at[3], {"tp": far})
+    copy_x.start()
+    own = projected[t] + core_in[x].astype(f32)
+    copy_x.wait()
+    turn_out[...] = (own + x_in[...].astype(f32)).astype(bf16)
+
+    @pl.when(d != t)
+    def _():
+        copy_turn = send(
+            turn_out, turn_in, hop_sems.at[4], hop_sems.at[5], {"dev": t, "tp": d}
+        )
+        copy_turn.start()
+        copy_turn.wait()
+
+    @pl.when(d == t)
+    def _():
+        turn_in[...] = turn_out[...]
+
+    mixed = res_ref[...].astype(f32) + turn_in[...].astype(f32)
+    mixed_ref[...] = mixed
+    gained = mixed * gain_ref[...]
+    lane = lax.broadcasted_iota(jnp.int32, (row_count, 128), 1)
+    stat = jnp.where(lane == experts, jnp.sum(mixed * mixed, 1, keepdims=True), 0.0)
+    router = router_ref[...].astype(f32)
+    for e in range(experts):
+        stat = jnp.where(
+            lane == e, jnp.sum(gained * router[e : e + 1, :], 1, keepdims=True), stat
+        )
+    stat_out[...] = stat
+    copies = []
+    for off in range(1, 4):
+        copy = send(
+            stat_out,
+            stat_in.at[off],
+            stat_sems.at[0, off],
+            stat_sems.at[1, off],
+            {"tp": lax.rem(t + off, 4)},
+        )
+        copy.start()
+        copies.append(copy)
+
+    first = routes_ref[:, 0:1]
+    second = routes_ref[:, 1:2]
+    first_hot = (lane == first).astype(f32)
+    second_hot = (lane == second).astype(f32)
+    row_i = lax.broadcasted_iota(jnp.int32, (row_count, row_count), 0)
+    row_j = lax.broadcasted_iota(jnp.int32, (row_count, row_count), 1)
+    place = jnp.dot(
+        (row_j < row_i).astype(bf16),
+        (first_hot + second_hot).astype(bf16),
+        preferred_element_type=f32,
+    )
+    first_place = jnp.sum(first_hot * place, 1, keepdims=True)
+    second_place = jnp.sum(second_hot * place, 1, keepdims=True)
+    wide_lane = lax.broadcasted_iota(jnp.int32, (row_count, experts * CAP), 1)
+    pick_first = (
+        wide_lane.astype(f32) == first.astype(f32) * CAP + first_place
+    ).astype(bf16)
+    pick_second = (
+        wide_lane.astype(f32) == second.astype(f32) * CAP + second_place
+    ).astype(bf16)
+    across = lax.broadcasted_iota(jnp.int32, (8, row_count), 0)
+    member_t = (across == routes_t_ref[0:1, :]).astype(f32) + (
+        across == routes_t_ref[1:2, :]
+    ).astype(f32)
+    place_t = jnp.dot(
+        member_t.astype(bf16), (row_i < row_j).astype(bf16), preferred_element_type=f32
+    )
+    slot = lax.broadcasted_iota(jnp.int32, (CAP, row_count), 0).astype(f32)
+    select = jnp.concatenate(
+        [
+            jnp.where(slot == place_t[e : e + 1, :], member_t[e : e + 1, :], 0.0)
+            for e in range(experts)
+        ],
+        0,
+    ).astype(bf16)
+
+    for copy in copies:
+        copy.wait()
+    stat = stat + stat_in[1] + stat_in[2] + stat_in[3]
+    square = jnp.sum(jnp.where(lane == experts, stat, 0.0), 1, keepdims=True)
+    scale_row = lax.rsqrt(square / D + eps)
+    logits = stat * scale_row
+    first_logit = jnp.sum(first_hot * logits, 1, keepdims=True)
+    second_logit = jnp.sum(second_hot * logits, 1, keepdims=True)
+    first_gate = 1.0 / (1.0 + jnp.exp(second_logit - first_logit))
+    second_gate = 1.0 / (1.0 + jnp.exp(first_logit - second_logit))
+    normed = (gained * scale_row).astype(bf16)
+    picked = jnp.dot(select, normed, preferred_element_type=f32)
+    for e in range(experts):
+        outgoing[e] = fold(picked[e * CAP : (e + 1) * CAP])
+    copies = []
+    for off in range(1, 4):
+        peer = lax.rem(d + off, 4)
+        copy = send(
+            outgoing.at[peer],
+            arrived.at[d],
+            there_sems.at[0, off],
+            there_sems.at[1, off],
+            {"dev": peer},
+        )
+        copy.start()
+        copies.append(copy)
+    arrived[d] = outgoing[d]
+    acc[...] = jnp.zeros_like(acc)
+    for copy in copies:
+        copy.wait()
+    flat_ref[...] = jnp.concatenate([unfold(arrived[s]) for s in range(4)], 0).astype(bf16)
+
+    def pair_copy(k):
+        return send(
+            pair_out.at[k], pair_in.at[k], pair_sems.at[0, k], pair_sems.at[1, k], {"tp": sibling}
+        )
+
+    def far_copy(k):
+        return send(
+            far_out.at[k], far_in.at[k], far_sems.at[0, k], far_sems.at[1, k], {"tp": far}
+        )
+
+    def hid_copy(k):
+        return send(
+            hid_own.at[k], hid_in.at[k], hid_sems.at[0, k], hid_sems.at[1, k], {"tp": sibling}
+        )
+
+    mine = pl.ds(pl.multiple_of(core * half, half), half)
+    others = pl.ds(pl.multiple_of((1 - core) * half, half), half)
+
+    @pl.loop(0, CHUNKS + 4)
+    def _(s):
+        @pl.when(s < CHUNKS)
+        def _():
+            k = s
+            up_copy(k).wait()
+            pair_out[k] = lax.dot_general(
+                flat_ref[...], weights[k, others, :], NT, preferred_element_type=f32
+            ).astype(bf16)
+            pair_copy(k).start()
+            own_pre[k] = lax.dot_general(
+                flat_ref[...], weights[k, mine, :], NT, preferred_element_type=f32
+            )
+
+            @pl.when(k < 2 * CHUNKS - slots)
+            def _():
+                down_copy(k + slots - CHUNKS).start()
+
+        @pl.when((s >= 1) & (s < CHUNKS + 1))
+        def _():
+            k = s - 1
+            pair_copy(k).wait()
+            both = own_pre[k] + pair_in[k].astype(f32)
+            own_pre[k] = both
+            far_out[k] = both.astype(bf16)
+            far_copy(k).start()
+
+        @pl.when((s >= 3) & (s < CHUNKS + 3))
+        def _():
+            k = s - 3
+            far_copy(k).wait()
+            pre = own_pre[k] + far_in[k].astype(f32)
+            hid_own[k] = (pre / (1.0 + jnp.exp(-pre))).astype(bf16)
+            hid_copy(k).start()
+
+        @pl.when(s >= 4)
+        def _():
+            k = s - 4
+            place_k = lax.rem(k + CHUNKS, slots)
+            down_copy(k).wait()
+            acc[...] += jnp.dot(
+                hid_own[k], weights[place_k, mine, :], preferred_element_type=f32
+            )
+            hid_copy(k).wait()
+            acc[...] += jnp.dot(
+                hid_in[k], weights[place_k, others, :], preferred_element_type=f32
+            )
+
+    for s in range(4):
+        back_out[s] = fold(acc[s * CAP : (s + 1) * CAP, :])
+    copies = []
+    for off in range(1, 4):
+        peer = lax.rem(d + off, 4)
+        copy = send(
+            back_out.at[peer],
+            back_in.at[d],
+            back_sems.at[0, off],
+            back_sems.at[1, off],
+            {"dev": peer},
+        )
+        copy.start()
+        copies.append(copy)
+    back_in[d] = back_out[d]
+    for copy in copies:
+        copy.wait()
+    returned = jnp.concatenate([unfold(back_in[s]) for s in range(4)], 0).astype(bf16)
+    out_ref[...] = (
+        mixed_ref[...]
+        + first_gate * jnp.dot(pick_first, returned, preferred_element_type=f32)
+        + second_gate * jnp.dot(pick_second, returned, preferred_element_type=f32)
+    ).astype(bf16)
+
+
+def fused_layer(
+    attention, residual_input, norm_gain, router_weight, routes, out_weight, up_weight, down_weight
+):
+    row_count, features = residual_input.shape
+    hidden = up_weight.shape[0]
+    chunk = hidden // CHUNKS
+    half = chunk // 2
+    rows = 4 * CAP
+    slots = 14
+    f32, bf16 = jnp.float32, jnp.bfloat16
+    vmem = pl.BlockSpec(memory_space=pltpu.VMEM)
+    hbm = pl.BlockSpec(memory_space=pl.ANY)
+    dma = pltpu.SemaphoreType.DMA
+    folded = (4, 2 * CAP, features // 2)
+    block = (row_count, features)
+    scratch = [
+        pltpu.VMEM((slots, chunk, features), bf16),
+        pltpu.VMEM(out_weight.shape, bf16),
+        pltpu.VMEM((4,) + block, bf16),
+        pltpu.VMEM((4,) + block, f32),
+        pltpu.VMEM((2,) + block, bf16),
+        pltpu.VMEM((2,) + block, bf16),
+        pltpu.VMEM(block, bf16),
+        pltpu.VMEM(block, bf16),
+        pltpu.VMEM(block, bf16),
+        pltpu.VMEM(block, bf16),
+        pltpu.VMEM(block, f32),
+        pltpu.VMEM((row_count, 128), f32),
+        pltpu.VMEM((4, row_count, 128), f32),
+        pltpu.VMEM(folded, bf16),
+        pltpu.VMEM(folded, bf16),
+        pltpu.VMEM((rows, features), bf16),
+        pltpu.VMEM((CHUNKS, rows, half), bf16),
+        pltpu.VMEM((CHUNKS, rows, half), bf16),
+        pltpu.VMEM((CHUNKS, rows, half), f32),
+        pltpu.VMEM((CHUNKS, rows, half), bf16),
+        pltpu.VMEM((CHUNKS, rows, half), bf16),
+        pltpu.VMEM((CHUNKS, rows, half), bf16),
+        pltpu.VMEM((CHUNKS, rows, half), bf16),
+        pltpu.VMEM((rows, features), f32),
+        pltpu.VMEM(folded, bf16),
+        pltpu.VMEM(folded, bf16),
+        dma((2 * CHUNKS,)),
+        dma,
+        dma((2, 4)),
+        dma((6,)),
+        dma((2, 4)),
+        dma((2, 4)),
+        dma((2, 4)),
+        dma((2, CHUNKS)),
+        dma((2, CHUNKS)),
+        dma((2, CHUNKS)),
+    ]
+    return pl.pallas_call(
+        layer_kernel,
+        out_shape=jax.ShapeDtypeStruct(block, bf16),
+        in_specs=[vmem] * 6 + [hbm] * 3,
+        out_specs=vmem,
+        scratch_shapes=scratch,
+        compiler_params=pltpu.CompilerParams(
+            collective_id=0, has_side_effects=True, vmem_limit_bytes=60 * 1024 * 1024
+        ),
+        cost_estimate=pl.CostEstimate(
+            flops=4 * rows * hidden * features,
+            bytes_accessed=4 * hidden * features + out_weight.size * 2,
+            transcendentals=rows * hidden,
+        ),
+    )(
+        attention,
+        residual_input,
+        norm_gain.reshape(1, features),
+        router_weight.T,
+        routes,
+        routes.T,
+        out_weight,
+        up_weight,
+        down_weight,
+    )
 
 
 def sum_heads(terms):
@@ -81,6 +520,17 @@
     attention = jnp.dot(placing, attention_slot, preferred_element_type=jnp.float32).astype(
         jnp.bfloat16
     )
+    if devices == 4 and lax.axis_size("tp") == 4 and experts == 4:
+        return fused_layer(
+            attention,
+            residual_input,
+            norm_gain,
+            router_weight,
+            routes,
+            out_weight,
+            up_weight,
+            down_weight,
+        )
     partial_rows = jnp.dot(
         lax.all_gather(attention, "dev", axis=0, tiled=True),
         out_weight,

time: 227 us -> 81.1 us (0.36)
  waiting for transfers between devices: 99.6 us -> 0 us
  Pallas kernels: 0 us -> 72 us
  blocking collectives: 63.7 us -> 0 us
  matrix products: 38.1 us -> 2.81 us
  between operations: 13.6 us -> 0.14 us
  starting transfers between devices: 4.62 us -> 0 us
    pallas_call x0 -> x1, Pallas kernels: none -> 72 us  [fused_layer(): pl.pallas_call(layer_kernel, out_shape=jax.ShapeDtypeStruct(block, bf16),...]
    psum x1 -> x0, waiting for transfers between devices: 67.6 us -> none  [body(): summed = lax.psum(pre, 'tp')]
    all_to_all x2 -> x0, blocking collectives: 36 us -> none  [the longest x1 21.8 us: body(): lax.all_to_all(partial_rows, 'dev', split_axis=0, concat_axis=1, tiled=True)]
    dot_general x6 -> x0, matrix products: 34.7 us -> none  [the longest x1 14.1 us: body(): lax.dot_general(flat, up_weight, (((1,), (1,)), ((), ())), preferred_elem...]
    reduce_scatter x1 -> x0, waiting for transfers between devices: 22.5 us -> none  [sum_heads(): return lax.psum_scatter(terms, 'tp', scatter_dimension=1, tiled=True)]
    all_gather x1 -> x0, blocking collectives: 16.2 us -> none  [body(): lax.all_gather(attention, 'dev', axis=0, tiled=True)]
    psum x2 -> x0, blocking collectives: 11.5 us -> none  [the longest x1 5.76 us: body(): square = lax.psum(jnp.sum(mixed * mixed, 1), 'tp')]
    all_to_all x1 -> x0, waiting for transfers between devices: 9.45 us -> none  [body(): lax.all_to_all(part.reshape(devices, count, features), 'dev', split_axis=...]
  transfers between devices with their start and end apart: 3 -> 0, of which waited for: 3 -> 0; matrix products, arithmetic and copies ran while one was open for 0% -> 0% of each run, Pallas kernels for 0% -> 0%
where the time goes in v1:
time: 81.1 us; the launch traced here: 80.9 us
  Pallas kernels  72 us (89%)
  local copies, waits for them, and re-layouts  5.44 us (7%)
  matrix products  2.81 us (3%)
    pallas_call x1, Pallas kernels, fused_layer(): pl.pallas_call(layer_kernel, out_shape=jax.ShapeDtypeStruct(block, bf16),...  72 us
    unnamed x15, local copies, waits for them, and re-layouts  2.27 us
    slice x1, local copies, waits for them, and re-layouts, body(): keys = cache[:, 0].reshape(row_count, positions, kv_local, HEAD_DIM)  1.72 us

profile of v1, /device:TPU:0, one launch (start us, length us, event | category | flops | bytes accessed | tf_op | source)
XLA Modules:
  0.0 80.9 jit_solution(17779106879425705661)
XLA Ops:
  0.0 0.0 copy-start
  0.0 0.0 copy-start.3
  0.0 0.0 copy-start.5
  0.0 0.0 copy-start.1
  0.0 1.7 %fusion.15 = (bf16[32,1,64,256]{3,2,1,0:T(8,128)(2,1)S(1)}, bf16[32,1,64,256]{3,2,1,0:T(8,128)(2,1)S(1)}) fusion(bf16[32,2,64,256]{3,2,1,0:T(8,128)(2,1)} %param.15), kind=kLoop, calls=%fused_computation.29 | loop fusion | bytes 4194304 | tf_op jit(solution)/shard_map/slice | solution.py:492
  1.7 0.3 reshape_squeeze.6
  2.0 0.0 copy-done
  2.0 0.0 copy-done.3
  2.1 0.3 convolution_convert_fusion.1
  2.3 0.1 reshape.46
  2.5 0.0 copy-done.5
  2.5 0.1 iota_compare_fusion
  2.6 0.8 fusion.16
  3.3 0.0 copy-done.1
  3.3 0.3 convolution_convert_fusion.2
  3.6 0.0 copy-start.4
  3.6 0.0 copy-start.2
  3.7 0.2 fusion.7
  3.9 0.3 fusion.4
  4.2 0.1 fusion.14
  4.3 0.3 reshape_squeeze.7
  4.6 0.5 fusion.1
  5.0 0.1 convert_element_type.43
  5.2 0.9 %convolution_convert_fusion.att_ref = bf16[32,1536]{1,0:T(8,128)(2,1)} fusion(bf16[32,1536]{1,0:T(8,128)(2,1)S(1)} %convert_element_type.43, s32[32]{0:T(128)S(1)} %copy-done.3), kind=kOutput, calls=%fused_computation | convolution fusion | flops 3195904 | bytes 196736 | tf_op jit(solution)/shard_map/dot_general | solution.py:520
  6.0 0.0 copy-done.4
  6.0 0.7 copy.16.routes_ref
  6.7 0.0 copy-done.2
  6.7 0.6 reshape.49.gain_ref
  7.3 72.0 %shard_map.118 = bf16[32,1536]{1,0:T(8,128)(2,1)} custom-call(bf16[32,1536]{1,0:T(8,128)(2,1)} %convolution_convert_fusion.att_ref, bf16[32,1536]{1,0:T(8,128)(2,1)} %res_ref.1, f32[1,1536]{1,0:T(1,128)} %reshape.49.gain_ref, bf16[4,1536]{1,0:T(4,128)(2,1)} %bitcast.27, s32[32,2]{1,0:T(8,128)} %copy.16.routes_ref, s32[2,32]{1,0:T(2,128)} %bitcast.28, ...), custom_call_target="tpu_custom_call" | custom-call | flops 4831838208 | bytes 55050240 | tf_op jit(solution)/shard_map/pallas_call | solution.py:426
  79.3 1.5 %copy.29 = bf16[32,1536]{1,0:T(8,128)(2,1)} copy(bf16[32,1536]{1,0:T(8,128)(2,1)} %shard_map.118) | data formatting | bytes 196608
  (4 shorter events, 0.1 us)
Async XLA Ops:
  0.0 2.0 %copy-start = (bf16[32,1536]{1,0:T(8,128)(2,1)S(1)}, bf16[32,1536]{1,0:T(8,128)(2,1)}, u32[]{:S(2)}) copy-start(bf16[32,1536]{1,0:T(8,128)(2,1)} %param.13) | copy-start | bytes 294916
  0.0 2.0 %copy-start.3 = (s32[32]{0:T(128)S(1)}, s32[32]{0:T(128)}, u32[]{:S(2)}) copy-start(s32[32]{0:T(128)} %param.17) | copy-start | bytes 388
  0.0 2.5 %copy-start.5 = (s32[32]{0:T(128)S(1)}, s32[32]{0:T(128)}, u32[]{:S(2)}) copy-start(s32[32]{0:T(128)} %param.16) | copy-start | bytes 388
  0.0 3.3 %copy-start.1 = (bf16[32,2,256]{2,1,0:T(2,128)(2,1)S(1)}, bf16[32,2,256]{2,1,0:T(2,128)(2,1)}, u32[]{:S(2)}) copy-start(bf16[32,2,256]{2,1,0:T(2,128)(2,1)} %param.14) | copy-start | bytes 98308
  3.6 2.4 %copy-start.4 = (s32[32,2]{0,1:T(2,128)S(1)}, s32[32,2]{0,1:T(2,128)}, u32[]{:S(2)}) copy-start(s32[32,2]{0,1:T(2,128)} %param.23) | copy-start | bytes 772
  3.6 3.1 %copy-start.2 = (f32[1536]{0:T(1024)S(1)}, f32[1536]{0:T(1024)}, u32[]{:S(2)}) copy-start(f32[1536]{0:T(1024)} %param.19) | copy-start | bytes 18436

commit v2 on v1

--- a/solution.py
+++ b/solution.py
@@ -45,7 +45,6 @@
     res_ref,
     gain_ref,
     router_ref,
-    routes_ref,
     routes_t_ref,
     outw_hbm,
     up_hbm,
@@ -157,40 +156,62 @@
 
     rows_all = gathered[...].reshape(devices * row_count, features)
 
-    @pl.loop(0, 3)
-    def _(j):
-        cols = pl.ds(pl.multiple_of(j * 512, 512), 512)
-        projected[:, :, cols] = jnp.dot(
+    cuts = core_out.shape[0]
+    width = features // cuts
+    core_copies = []
+    for j in range(cuts):
+        cols = slice(j * width, (j + 1) * width)
+        projected[j] = jnp.dot(
             rows_all, outw[:, cols], preferred_element_type=f32
-        ).reshape(devices, row_count, 512)
-
-    core_out[0] = projected[1 - core].astype(bf16)
-    core_out[1] = projected[3 - core].astype(bf16)
-    copy_core = send(core_out, core_in, hop_sems.at[0], hop_sems.at[1], {"tp": sibling})
-    copy_core.start()
-    copy_core.wait()
-    x_out[...] = (projected[far] + core_in[1 - x].astype(f32)).astype(bf16)
-    copy_x = send(x_out, x_in, hop_sems.at[2], hop_sems.at[3], {"tp": far})
-    copy_x.start()
-    own = projected[t] + core_in[x].astype(f32)
-    copy_x.wait()
-    turn_out[...] = (own + x_in[...].astype(f32)).astype(bf16)
+        ).reshape(devices, row_count, width)
+        core_out[j, 0] = projected[j, 1 - core].astype(bf16)
+        core_out[j, 1] = projected[j, 3 - core].astype(bf16)
+        copy = send(
+            core_out.at[j], core_in.at[j], hop_sems.at[0, j], hop_sems.at[1, j], {"tp": sibling}
+        )
+        copy.start()
+        core_copies.append(copy)
+    x_copies = []
+    for j in range(cuts):
+        core_copies[j].wait()
+        x_out[j] = (projected[j, far] + core_in[j, 1 - x].astype(f32)).astype(bf16)
+        copy = send(x_out.at[j], x_in.at[j], hop_sems.at[2, j], hop_sems.at[3, j], {"tp": far})
+        copy.start()
+        x_copies.append(copy)
+
+    def turn_copy(j):
+        return send(
+            turn_out.at[j],
+            turn_in.at[j],
+            hop_sems.at[4, j],
+            hop_sems.at[5, j],
+            {"dev": t, "tp": d},
+        )
+
+    for j in range(cuts):
+        x_copies[j].wait()
+        turn_out[j] = (
+            projected[j, t] + core_in[j, x].astype(f32) + x_in[j].astype(f32)
+        ).astype(bf16)
+
+        @pl.when(d != t)
+        def _():
+            turn_copy(j).start()
+
+        @pl.when(d == t)
+        def _():
+            turn_in[j] = turn_out[j]
 
     @pl.when(d != t)
     def _():
-        copy_turn = send(
-            turn_out, turn_in, hop_sems.at[4], hop_sems.at[5], {"dev": t, "tp": d}
-        )
-        copy_turn.start()
-        copy_turn.wait()
-
-    @pl.when(d == t)
-    def _():
-        turn_in[...] = turn_out[...]
-
-    mixed = res_ref[...].astype(f32) + turn_in[...].astype(f32)
+        for j in range(cuts):
+            turn_copy(j).wait()
+
+    turned = jnp.concatenate([turn_in[j] for j in range(cuts)], 1)
+    mixed = res_ref[...].astype(f32) + turned.astype(f32)
     mixed_ref[...] = mixed
-    gained = mixed * gain_ref[...]
+    gain = jnp.concatenate([gain_ref[i : i + 1, :] for i in range(gain_ref.shape[0])], 1)
+    gained = mixed * gain
     lane = lax.broadcasted_iota(jnp.int32, (row_count, 128), 1)
     stat = jnp.where(lane == experts, jnp.sum(mixed * mixed, 1, keepdims=True), 0.0)
     router = router_ref[...].astype(f32)
@@ -211,12 +232,14 @@
         copy.start()
         copies.append(copy)
 
-    first = routes_ref[:, 0:1]
-    second = routes_ref[:, 1:2]
-    first_hot = (lane == first).astype(f32)
-    second_hot = (lane == second).astype(f32)
     row_i = lax.broadcasted_iota(jnp.int32, (row_count, row_count), 0)
     row_j = lax.broadcasted_iota(jnp.int32, (row_count, row_count), 1)
+    same = row_i == row_j
+    routes_wide = routes_t_ref[...].astype(f32)
+    first = jnp.sum(jnp.where(same, routes_wide[0:1, :], 0.0), 1, keepdims=True)
+    second = jnp.sum(jnp.where(same, routes_wide[1:2, :], 0.0), 1, keepdims=True)
+    first_hot = (lane.astype(f32) == first).astype(f32)
+    second_hot = (lane.astype(f32) == second).astype(f32)
     place = jnp.dot(
         (row_j < row_i).astype(bf16),
         (first_hot + second_hot).astype(bf16),
@@ -226,10 +249,10 @@
     second_place = jnp.sum(second_hot * place, 1, keepdims=True)
     wide_lane = lax.broadcasted_iota(jnp.int32, (row_count, experts * CAP), 1)
     pick_first = (
-        wide_lane.astype(f32) == first.astype(f32) * CAP + first_place
+        wide_lane.astype(f32) == first * CAP + first_place
     ).astype(bf16)
     pick_second = (
-        wide_lane.astype(f32) == second.astype(f32) * CAP + second_place
+        wide_lane.astype(f32) == second * CAP + second_place
     ).astype(bf16)
     across = lax.broadcasted_iota(jnp.int32, (8, row_count), 0)
     member_t = (across == routes_t_ref[0:1, :]).astype(f32) + (
@@ -385,17 +408,19 @@
     dma = pltpu.SemaphoreType.DMA
     folded = (4, 2 * CAP, features // 2)
     block = (row_count, features)
+    cuts = 3
+    piece = (row_count, features // cuts)
     scratch = [
         pltpu.VMEM((slots, chunk, features), bf16),
         pltpu.VMEM(out_weight.shape, bf16),
         pltpu.VMEM((4,) + block, bf16),
-        pltpu.VMEM((4,) + block, f32),
-        pltpu.VMEM((2,) + block, bf16),
-        pltpu.VMEM((2,) + block, bf16),
-        pltpu.VMEM(block, bf16),
-        pltpu.VMEM(block, bf16),
-        pltpu.VMEM(block, bf16),
-        pltpu.VMEM(block, bf16),
+        pltpu.VMEM((cuts, 4) + piece, f32),
+        pltpu.VMEM((cuts, 2) + piece, bf16),
+        pltpu.VMEM((cuts, 2) + piece, bf16),
+        pltpu.VMEM((cuts,) + piece, bf16),
+        pltpu.VMEM((cuts,) + piece, bf16),
+        pltpu.VMEM((cuts,) + piece, bf16),
+        pltpu.VMEM((cuts,) + piece, bf16),
         pltpu.VMEM(block, f32),
         pltpu.VMEM((row_count, 128), f32),
         pltpu.VMEM((4, row_count, 128), f32),
@@ -415,7 +440,7 @@
         dma((2 * CHUNKS,)),
         dma,
         dma((2, 4)),
-        dma((6,)),
+        dma((6, cuts)),
         dma((2, 4)),
         dma((2, 4)),
         dma((2, 4)),
@@ -426,7 +451,7 @@
     return pl.pallas_call(
         layer_kernel,
         out_shape=jax.ShapeDtypeStruct(block, bf16),
-        in_specs=[vmem] * 6 + [hbm] * 3,
+        in_specs=[vmem] * 5 + [hbm] * 3,
         out_specs=vmem,
         scratch_shapes=scratch,
         compiler_params=pltpu.CompilerParams(
@@ -440,9 +465,8 @@
     )(
         attention,
         residual_input,
-        norm_gain.reshape(1, features),
+        norm_gain.reshape(features // 128, 128),
         router_weight.T,
-        routes,
         routes.T,
         out_weight,
         up_weight,

time: 81.1 us -> 77.4 us (0.954)
  Pallas kernels: 72 us -> 69.3 us
  local copies, waits for them, and re-layouts: 5.44 us -> 4.15 us
    pallas_call x1, Pallas kernels: 72 us -> 69.3 us  [fused_layer(): pl.pallas_call(layer_kernel, out_shape=jax.ShapeDtypeStruct(block, bf16),...]
    unnamed x15 -> x10, local copies, waits for them, and re-layouts: 2.27 us -> 1.57 us
where the time goes in v2:
time: 77.4 us; the launch traced here: 76.8 us
  Pallas kernels  69.3 us (90%)
  local copies, waits for them, and re-layouts  4.15 us (5%)
  matrix products  2.81 us (4%)
    pallas_call x1, Pallas kernels, fused_layer(): pl.pallas_call(layer_kernel, out_shape=jax.ShapeDtypeStruct(block, bf16),...  69.3 us
    slice x1, local copies, waits for them, and re-layouts, body(): keys = cache[:, 0].reshape(row_count, positions, kv_local, HEAD_DIM)  1.72 us
    unnamed x10, local copies, waits for them, and re-layouts  1.57 us

profile of v2, /device:TPU:0, one launch (start us, length us, event | category | flops | bytes accessed | tf_op | source)
XLA Modules:
  0.0 76.8 jit_solution(15216933974125373646)
XLA Ops:
  0.0 0.0 copy-start
  0.0 0.0 copy-start.2
  0.0 0.0 copy-start.3
  0.0 0.0 copy-start.1
  0.0 1.7 %fusion.15 = (bf16[32,1,64,256]{3,2,1,0:T(8,128)(2,1)S(1)}, bf16[32,1,64,256]{3,2,1,0:T(8,128)(2,1)S(1)}) fusion(bf16[32,2,64,256]{3,2,1,0:T(8,128)(2,1)} %param.15), kind=kLoop, calls=%fused_computation.29 | loop fusion | bytes 4194304 | tf_op jit(solution)/shard_map/slice | solution.py:516
  1.7 0.3 reshape_squeeze.6
  2.0 0.0 copy-done
  2.0 0.0 copy-done.2
  2.1 0.3 convolution_convert_fusion.1
  2.3 0.1 reshape.46
  2.5 0.0 copy-done.3
  2.5 0.1 iota_compare_fusion
  2.6 0.8 fusion.16
  3.3 0.0 copy-done.1
  3.3 0.3 convolution_convert_fusion.2
  3.7 0.2 fusion.7
  3.9 0.3 fusion.4
  4.2 0.1 fusion.14
  4.2 0.3 reshape_squeeze.7
  4.5 0.5 fusion.1
  5.0 0.1 convert_element_type.43
  5.1 0.9 %convolution_convert_fusion.att_ref = bf16[32,1536]{1,0:T(8,128)(2,1)} fusion(bf16[32,1536]{1,0:T(8,128)(2,1)S(1)} %convert_element_type.43, s32[32]{0:T(128)S(1)} %copy-done.2), kind=kOutput, calls=%fused_computation | convolution fusion | flops 3195904 | bytes 196736 | tf_op jit(solution)/shard_map/dot_general | solution.py:544
  6.0 69.3 %shard_map.118 = bf16[32,1536]{1,0:T(8,128)(2,1)} custom-call(bf16[32,1536]{1,0:T(8,128)(2,1)} %convolution_convert_fusion.att_ref, bf16[32,1536]{1,0:T(8,128)(2,1)} %res_ref.1, f32[12,128]{1,0:T(8,128)} %bitcast.29, bf16[4,1536]{1,0:T(4,128)(2,1)} %bitcast.28, s32[2,32]{1,0:T(2,128)} %bitcast.30, bf16[1536,1536]{1,0:T(8,128)(2,1)} %outw_hbm.1, ...), custom_call_target="tpu_custom_call" | custom-call | flops 4831838208 | bytes 55050240 | tf_op jit(solution)/shard_map/pallas_call | solution.py:451
  75.3 1.5 %copy.27 = bf16[32,1536]{1,0:T(8,128)(2,1)} copy(bf16[32,1536]{1,0:T(8,128)(2,1)} %shard_map.118) | data formatting | bytes 196608
  (4 shorter events, 0.1 us)
Async XLA Ops:
  0.0 2.0 %copy-start = (bf16[32,1536]{1,0:T(8,128)(2,1)S(1)}, bf16[32,1536]{1,0:T(8,128)(2,1)}, u32[]{:S(2)}) copy-start(bf16[32,1536]{1,0:T(8,128)(2,1)} %param.13) | copy-start | bytes 294916
  0.0 2.0 %copy-start.2 = (s32[32]{0:T(128)S(1)}, s32[32]{0:T(128)}, u32[]{:S(2)}) copy-start(s32[32]{0:T(128)} %param.17) | copy-start | bytes 388
  0.0 2.5 %copy-start.3 = (s32[32]{0:T(128)S(1)}, s32[32]{0:T(128)}, u32[]{:S(2)}) copy-start(s32[32]{0:T(128)} %param.16) | copy-start | bytes 388
  0.0 3.3 %copy-start.1 = (bf16[32,2,256]{2,1,0:T(2,128)(2,1)S(1)}, bf16[32,2,256]{2,1,0:T(2,128)(2,1)}, u32[]{:S(2)}) copy-start(bf16[32,2,256]{2,1,0:T(2,128)(2,1)} %param.14) | copy-start | bytes 98308

commit v3 on v2

--- a/solution.py
+++ b/solution.py
@@ -41,7 +41,8 @@
 
 
 def layer_kernel(
-    att_ref,
+    slots_ref,
+    att_slot_ref,
     res_ref,
     gain_ref,
     router_ref,
@@ -52,6 +53,7 @@
     out_ref,
     weights,
     outw,
+    att_ref,
     gathered,
     projected,
     core_out,
@@ -132,6 +134,20 @@
     @pl.when(d != t)
     def _():
         pl.semaphore_signal(barrier, inc=1, device_id={"dev": t, "tp": d}, device_id_type=MESH)
+
+    row_i = lax.broadcasted_iota(jnp.int32, (row_count, row_count), 0)
+    row_j = lax.broadcasted_iota(jnp.int32, (row_count, row_count), 1)
+    same = row_i == row_j
+    row_slot = jnp.sum(
+        jnp.where(same, slots_ref[...].astype(f32), 0.0), 1, keepdims=True
+    )
+    placing = (row_j.astype(f32) == row_slot).astype(bf16)
+    placed = jnp.dot(placing, att_slot_ref[...], preferred_element_type=f32).astype(bf16)
+    att_ref[...] = placed
+    gathered[d] = placed
+
+    @pl.when(d != t)
+    def _():
         pl.semaphore_wait(barrier, 7)
 
     @pl.when(d == t)
@@ -149,7 +165,6 @@
         )
         copy.start()
         copies.append(copy)
-    gathered[d] = att_ref[...]
     outw_copy.wait()
     for copy in copies:
         copy.wait()
@@ -232,9 +247,6 @@
         copy.start()
         copies.append(copy)
 
-    row_i = lax.broadcasted_iota(jnp.int32, (row_count, row_count), 0)
-    row_j = lax.broadcasted_iota(jnp.int32, (row_count, row_count), 1)
-    same = row_i == row_j
     routes_wide = routes_t_ref[...].astype(f32)
     first = jnp.sum(jnp.where(same, routes_wide[0:1, :], 0.0), 1, keepdims=True)
     second = jnp.sum(jnp.where(same, routes_wide[1:2, :], 0.0), 1, keepdims=True)
@@ -322,6 +334,15 @@
 
     @pl.loop(0, CHUNKS + 4)
     def _(s):
+        @pl.when((s >= 1) & (s < CHUNKS + 1))
+        def _():
+            k = s - 1
+            pair_copy(k).wait()
+            both = own_pre[k] + pair_in[k].astype(f32)
+            own_pre[k] = both
+            far_out[k] = both.astype(bf16)
+            far_copy(k).start()
+
         @pl.when(s < CHUNKS)
         def _():
             k = s
@@ -337,15 +358,6 @@
             @pl.when(k < 2 * CHUNKS - slots)
             def _():
                 down_copy(k + slots - CHUNKS).start()
-
-        @pl.when((s >= 1) & (s < CHUNKS + 1))
-        def _():
-            k = s - 1
-            pair_copy(k).wait()
-            both = own_pre[k] + pair_in[k].astype(f32)
-            own_pre[k] = both
-            far_out[k] = both.astype(bf16)
-            far_copy(k).start()
 
         @pl.when((s >= 3) & (s < CHUNKS + 3))
         def _():
@@ -394,7 +406,7 @@
 
 
 def fused_layer(
-    attention, residual_input, norm_gain, router_weight, routes, out_weight, up_weight, down_weight
+    slot_of, attention, residual_input, norm_gain, router_weight, routes, out_weight, up_weight, down_weight
 ):
     row_count, features = residual_input.shape
     hidden = up_weight.shape[0]
@@ -413,6 +425,7 @@
     scratch = [
         pltpu.VMEM((slots, chunk, features), bf16),
         pltpu.VMEM(out_weight.shape, bf16),
+        pltpu.VMEM(block, bf16),
         pltpu.VMEM((4,) + block, bf16),
         pltpu.VMEM((cuts, 4) + piece, f32),
         pltpu.VMEM((cuts, 2) + piece, bf16),
@@ -451,7 +464,7 @@
     return pl.pallas_call(
         layer_kernel,
         out_shape=jax.ShapeDtypeStruct(block, bf16),
-        in_specs=[vmem] * 5 + [hbm] * 3,
+        in_specs=[vmem] * 6 + [hbm] * 3,
         out_specs=vmem,
         scratch_shapes=scratch,
         compiler_params=pltpu.CompilerParams(
@@ -463,6 +476,7 @@
             transcendentals=rows * hidden,
         ),
     )(
+        slot_of.reshape(1, row_count),
         attention,
         residual_input,
         norm_gain.reshape(features // 128, 128),
@@ -541,12 +555,10 @@
         * current_slot[:, 1].astype(jnp.float32)[:, :, None, :]
     )
     attention_slot = attended.reshape(row_count, -1).astype(jnp.bfloat16)
-    attention = jnp.dot(placing, attention_slot, preferred_element_type=jnp.float32).astype(
-        jnp.bfloat16
-    )
     if devices == 4 and lax.axis_size("tp") == 4 and experts == 4:
         return fused_layer(
-            attention,
+            slots,
+            attention_slot,
             residual_input,
             norm_gain,
             router_weight,
@@ -555,6 +567,9 @@
             up_weight,
             down_weight,
         )
+    attention = jnp.dot(placing, attention_slot, preferred_element_type=jnp.float32).astype(
+        jnp.bfloat16
+    )
     partial_rows = jnp.dot(
         lax.all_gather(attention, "dev", axis=0, tiled=True),
         out_weight,

time: 77.4 us -> 76.2 us (0.984)
  matrix products: 2.81 us -> 1.95 us
    dot_general x1 -> x0, matrix products: 0.86 us -> none  [body(): jnp.dot(placing, attention_slot, preferred_element_type=jnp.float32)]
where the time goes in v3:
time: 76.2 us; the launch traced here: 76 us
  Pallas kernels  68.7 us (90%)
  local copies, waits for them, and re-layouts  4.79 us (6%)
  matrix products  1.95 us (3%)
    pallas_call x1, Pallas kernels, fused_layer(): pl.pallas_call(layer_kernel, out_shape=jax.ShapeDtypeStruct(block, bf16),...  68.7 us
    slice x1, local copies, waits for them, and re-layouts, body(): keys = cache[:, 0].reshape(row_count, positions, kv_local, HEAD_DIM)  1.72 us
    unnamed x10, local copies, waits for them, and re-layouts  1.57 us

profile of v3, /device:TPU:0, one launch (start us, length us, event | category | flops | bytes accessed | tf_op | source)
XLA Modules:
  0.0 76.0 jit_solution(4709516306781732309)
XLA Ops:
  0.0 0.0 copy-start
  0.0 0.0 copy-start.2
  0.0 0.0 copy-start.3
  0.0 0.0 copy-start.1
  0.0 1.7 %fusion.14 = (bf16[32,1,64,256]{3,2,1,0:T(8,128)(2,1)S(1)}, bf16[32,1,64,256]{3,2,1,0:T(8,128)(2,1)S(1)}) fusion(bf16[32,2,64,256]{3,2,1,0:T(8,128)(2,1)} %param.15), kind=kLoop, calls=%fused_computation.27 | loop fusion | bytes 4194304 | tf_op jit(solution)/shard_map/slice | solution.py:530
  1.7 0.3 reshape_squeeze.6
  2.0 0.0 copy-done
  2.0 0.0 copy-done.2
  2.1 0.3 convolution_convert_fusion
  2.3 0.1 reshape.50
  2.5 0.0 copy-done.3
  2.5 0.1 iota_compare_fusion.3
  2.6 0.8 %fusion.15 = (f32[32,2,6]{2,1,0:T(2,128)S(1)}, f32[32,2,6,64]{3,2,1,0:T(8,128)S(1)}) fusion(bf16[32,2,6,128]{3,2,1,0:T(8,128)(2,1)S(1)} %reshape.50, bf16[32,64,2,128]{3,2,1,0:T(2,128)(2,1)S(1)} %reshape_squeeze.6, pred[32,64]{1,0:T(8,128)(4,1)S(1)} %iota_compare_fusion.3), kind=kOutput, calls=%fused_computation.28 | convolution fusion | flops 6364800 | bytes 1248768 | tf_op jit(solution)/shard_map/bkgd,blkd->bkgl/dot_general | solution.py:534
  3.3 0.0 copy-done.1
  3.3 0.3 convolution_convert_fusion.1
  3.7 0.2 fusion.7
  3.9 0.3 fusion.4
  4.2 0.1 fusion.13
  4.2 0.3 reshape_squeeze.7
  4.5 0.5 fusion.1
  5.0 0.8 %convert_element_type.39.att_slot_ref = bf16[32,1536]{1,0:T(8,128)(2,1)} reshape(bf16[32,2,6,128]{3,2,1,0:T(8,128)(2,1)S(1)} %fusion.1) | data formatting | bytes 196608 | tf_op jit(solution)/shard_map/convert_element_type | solution.py:557
  5.8 68.7 %shard_map.118 = bf16[32,1536]{1,0:T(8,128)(2,1)} custom-call(s32[1,32]{1,0:T(1,128)} %bitcast.30, bf16[32,1536]{1,0:T(8,128)(2,1)} %convert_element_type.39.att_slot_ref, bf16[32,1536]{1,0:T(8,128)(2,1)} %res_ref.1, f32[12,128]{1,0:T(8,128)} %bitcast.29, bf16[4,1536]{1,0:T(4,128)(2,1)} %bitcast.28, s32[2,32]{1,0:T(2,128)} %bitcast.31, ...), custom_call_target="tpu_custom_call" | custom-call | flops 4831838208 | bytes 55050240 | tf_op jit(solution)/shard_map/pallas_call | solution.py:464
  74.4 1.5 %copy.27 = bf16[32,1536]{1,0:T(8,128)(2,1)} copy(bf16[32,1536]{1,0:T(8,128)(2,1)} %shard_map.118) | data formatting | bytes 196608
  (4 shorter events, 0.1 us)
Async XLA Ops:
  0.0 2.0 %copy-start = (bf16[32,1536]{1,0:T(8,128)(2,1)S(1)}, bf16[32,1536]{1,0:T(8,128)(2,1)}, u32[]{:S(2)}) copy-start(bf16[32,1536]{1,0:T(8,128)(2,1)} %param.13) | copy-start | bytes 294916
  0.0 2.0 %copy-start.2 = (s32[32]{0:T(128)S(1)}, s32[32]{0:T(128)}, u32[]{:S(2)}) copy-start(s32[32]{0:T(128)} %param.17) | copy-start | bytes 388
  0.0 2.5 %copy-start.3 = (s32[32]{0:T(128)S(1)}, s32[32]{0:T(128)}, u32[]{:S(2)}) copy-start(s32[32]{0:T(128)} %param.16) | copy-start | bytes 388
  0.0 3.3 %copy-start.1 = (bf16[32,2,256]{2,1,0:T(2,128)(2,1)S(1)}, bf16[32,2,256]{2,1,0:T(2,128)(2,1)}, u32[]{:S(2)}) copy-start(bf16[32,2,256]{2,1,0:T(2,128)(2,1)} %param.14) | copy-start | bytes 98308
